TPU v7x, 768 devices: a whole 4x8x12 slice. The times are simulated.
768 devices in a mesh: blk: 192 (over y_lo, z, x), grp: 4 (over y_hi, core).
Axes of the slice: x: 4, y: 8 (y_hi: 2, y_lo: 4; y = y_hi * 4 + y_lo), z: 12, core: 2. Of those that a mesh axis runs over, the one named last changes fastest.
Arguments:
- images: bfloat16 [196608, 1152], P(('blk', 'grp')), may hold values from -6 to 6
- texts: bfloat16 [196608, 1152], P(('blk', 'grp')), may hold values from -6 to 6
- row_weight: float32 [196608], P('blk'), may hold values from 0.05 to 0.5
- log_sharpness_parameter: float32 [1], replicated, may hold values from 2.3 to 2.9
- bias: float32 [1], replicated, may hold values from -2 to -0.5
Outputs:
- image_grad: float32 [196608, 1152], P(('blk', 'grp'))
- text_grad: bfloat16 [196608, 1152], P(('blk', 'grp'))
- row_loss: float32 [196608], P(('blk', 'grp'))
All inputs are finite; a program needn't handle non-finite values.
Results may differ from a plain program's by a relative error of at most 0.015.
Values may be sent and summed in bfloat16 or wider, within the bound.
A program may use at most 64 MiB of HBM per device.

v0:
```python
import jax
import jax.numpy as jnp
from jax import lax
from jax.sharding import PartitionSpec as P

STEPS = 2


def from_behind(value, axis, by):
    devices = lax.axis_size(axis)
    return lax.ppermute(value, axis, [(i, (i + by) % devices) for i in range(devices)])


def unit_rows(raw):
    values = raw.astype(jnp.float32)
    inverse = lax.rsqrt(jnp.sum(values * values, axis=-1, keepdims=True) + 1e-06)
    return (values * inverse, inverse)


def pass_on(carried, partial_sum):
    return from_behind((carried, partial_sum), "blk", 1)


def pairwise_terms(
    picture_segment_entries,
    caption_segment_entries,
    image_first_row,
    text_first_row,
    model_weights,
    sharpness_factor,
    segment_start_index,
):
    affinity_scores_matrix = (
        sharpness_factor
        * lax.dot_general(
            picture_segment_entries,
            caption_segment_entries,
            (((1,), (1,)), ((), ())),
            preferred_element_type=jnp.float32,
        )
        + segment_start_index
    )
    image_index = image_first_row + jnp.arange(picture_segment_entries.shape[0], dtype=jnp.int32)
    text_index = text_first_row + jnp.arange(caption_segment_entries.shape[0], dtype=jnp.int32)
    positive = (image_index[:, None] == text_index[None, :]).astype(jnp.float32)
    losses = jnp.sum(jax.nn.softplus((1.0 - 2.0 * positive) * affinity_scores_matrix), axis=1)
    grad_logit = (
        model_weights[:, None] * (jax.nn.sigmoid(affinity_scores_matrix) - positive)
    ).astype(jnp.bfloat16)
    return (losses, grad_logit)


def local(images, texts, row_weight, log_sharpness_parameter, bias):
    shard_rows, features = images.shape
    groups = lax.axis_size("blk")
    members = lax.axis_size("grp")
    position = lax.axis_index("blk")
    member = lax.axis_index("grp")
    group_rows = shard_rows * members
    sharpness_factor = jnp.exp(log_sharpness_parameter[0])
    segment_start_index = bias[0]
    normed, inverse = unit_rows(images)
    normed_b = normed.astype(jnp.bfloat16)
    carried = unit_rows(texts)[0].astype(jnp.bfloat16)
    partial_sum = jnp.zeros((shard_rows, features), jnp.bfloat16)
    own_weights = lax.dynamic_slice_in_dim(row_weight, member * shard_rows, shard_rows, 0)
    image_first_row = (position * members + member) * shard_rows
    negative_gradient_direction = jnp.zeros((shard_rows, features), jnp.float32)
    loss_sum = jnp.zeros((shard_rows,), jnp.float32)
    for visit in range(STEPS):
        source = (position - visit) % groups
        gathered_text = lax.all_gather(carried, "grp", axis=0, tiled=True)
        losses, grad_logit = pairwise_terms(
            normed_b,
            gathered_text,
            image_first_row,
            source * group_rows,
            own_weights,
            sharpness_factor,
            segment_start_index,
        )
        loss_sum = loss_sum + losses
        negative_gradient_direction = negative_gradient_direction + jnp.dot(
            grad_logit, gathered_text, preferred_element_type=jnp.float32
        )
        accumulated_cost_share = sharpness_factor * lax.dot_general(
            grad_logit, normed_b, (((0,), (0,)), ((), ())), preferred_element_type=jnp.float32
        )
        summed = lax.psum_scatter(
            accumulated_cost_share.astype(jnp.bfloat16), "grp", scatter_dimension=0, tiled=True
        ).astype(jnp.float32)
        partial_sum = (partial_sum.astype(jnp.float32) + summed).astype(jnp.bfloat16)
        if visit + 1 < STEPS:
            carried, partial_sum = pass_on(carried, partial_sum)
    multiplied_gradient_step = sharpness_factor * negative_gradient_direction
    image_grad = inverse * (
        multiplied_gradient_step
        - normed * jnp.sum(normed * multiplied_gradient_step, axis=-1, keepdims=True)
    )
    row_loss = loss_sum / (STEPS * group_rows)
    return (image_grad, partial_sum, row_loss)


def solution(mesh):
    placed = (P(("blk", "grp"), None), P(("blk", "grp"), None), P("blk"), P(), P())
    return jax.shard_map(
        local,
        mesh=mesh,
        in_specs=placed,
        out_specs=(P(("blk", "grp"), None), P(("blk", "grp"), None), P(("blk", "grp"))),
        check_vma=False,
    )
```

profile of v0, /device:TPU:1, one launch (start us, length us, event | category | flops | bytes accessed | tf_op | source)
XLA Modules:
  0.0 271.5 jit_solution(9860430112941511523)
XLA Ops:
  7.2 1.3 fusion.12
  8.5 2.1 fusion.13
  10.7 3.9 %collective-permute-start = (bf16[256,1152]{1,0:T(8,128)(2,1)}, bf16[256,1152]{1,0:T(8,128)(2,1)S(1)}, u32[]{:S(2)}, u32[]{:S(2)}) collective-permute-start(bf16[256,1152]{1,0:T(8,128)(2,1)} %fusion.13), channel_id=1, source_target_pairs={{0,4},{4,8},{8,12},{12,16},{16,20},{20,24},{24,28},{28,32},{32,36}... | collective-permute-start | bytes 1769480 | tf_op jit(solution)/shard_map/ppermute | solution.py:11
  14.6 29.7 %collective-permute-done = bf16[256,1152]{1,0:T(8,128)(2,1)S(1)} collective-permute-done((bf16[256,1152]{1,0:T(8,128)(2,1)}, bf16[256,1152]{1,0:T(8,128)(2,1)S(1)}, u32[]{:S(2)}, u32[]{:S(2)}) %collective-permute-start) | collective-permute-done | bytes 589856 | tf_op jit(solution)/shard_map/ppermute | solution.py:11
  44.3 0.8 copy-done.1
  45.1 0.0 reduce-scatter.3.cloned.1.call-start
  46.6 0.8 dynamic_slice.3
  47.3 0.2 fusion.11
  47.5 22.8 %all-gather.3.cloned.1.call-done = bf16[1024,1152]{1,0:T(8,128)(2,1)} async-done(((bf16[256,1152]{1,0:T(8,128)(2,1)}), bf16[1024,1152]{1,0:T(8,128)(2,1)}) %all-gather.3.cloned.1.call-update) | async-done | bytes 2359312 | tf_op jit(solution)/shard_map/all_gather | solution.py:72
  70.4 2.6 fusion.7
  72.9 2.6 fusion
  75.6 45.0 %all-gather.5.cloned.1.call-done = bf16[1024,1152]{1,0:T(8,128)(2,1)} async-done(((bf16[256,1152]{1,0:T(8,128)(2,1)}), bf16[1024,1152]{1,0:T(8,128)(2,1)}) %all-gather.5.cloned.1.call-update) | async-done | bytes 2359312 | tf_op jit(solution)/shard_map/all_gather | solution.py:72
  120.6 3.9 %fusion.25 = (f32[256]{0:T(256)S(1)}, f32[256]{0:T(256)S(1)}, f32[256,1024]{1,0:T(8,128)S(1)}) fusion(s32[1024]{0:T(1024)S(1)} %iota_add_fusion, s32[256]{0:T(256)S(1)} %iota_add_fusion.2, f32[256,1024]{1,0:T(8,128)S(1)} %fusion.7, s32[1024]{0:T(1024)S(1)} %iota_add_fusion.1, f32[]{:T(128)} %bitcast.7, bf16[1024,1152]{1,0:T(8,128)(2,1)} %all-gather.5.cloned.1.call-done, ...), kind=kOutput, calls=%fused_computation.41 | convolution fusion | flops 611155456 | bytes 5058568 | tf_op jit(solution)/shard_map/dot_general | solution.py:35
  124.6 1.0 copy-done.5
  125.5 2.6 fusion.1
  128.2 1.6 copy-done.2
  129.8 2.3 fusion.33
  132.2 1.1 fusion.8
  133.3 58.2 %reduce-scatter.3.cloned.1.call-done = bf16[256,1152]{1,0:T(8,128)(2,1)} async-done(((bf16[1024,1152]{1,0:T(8,128)(2,1)}), bf16[256,1152]{1,0:T(8,128)(2,1)}) %reduce-scatter.3.cloned.1.call-update) | async-done | bytes 589840 | tf_op jit(solution)/shard_map/reduce_scatter | solution.py:89
  191.5 1.9 collective-permute-start.1
  193.4 0.6 add_multiply_fusion
  194.0 1.3 fusion.10
  195.2 67.7 %reduce-scatter.5.cloned.1.call-done = bf16[256,1152]{1,0:T(8,128)(2,1)} async-done(((bf16[1024,1152]{1,0:T(8,128)(2,1)}), bf16[256,1152]{1,0:T(8,128)(2,1)}) %reduce-scatter.5.cloned.1.call-update) | async-done | bytes 589840 | tf_op jit(solution)/shard_map/reduce_scatter | solution.py:89
  263.0 2.0 add_convert_fusion
  (24 shorter events, 0.2 us)
Async XLA Ops:
  7.2 63.2 %all-gather.3.cloned.1.call-start = ((), (), s32[]{:S(2)}) async-start(), calls=%async_computation.2 | async-start | bytes 2949120 | tf_op jit(solution)/shard_map/all_gather | solution.py:72
  8.5 38.8 %copy-start = (bf16[256,1152]{1,0:T(8,128)(2,1)S(1)}, bf16[256,1152]{1,0:T(8,128)(2,1)}, u32[]{:S(2)}) copy-start(bf16[256,1152]{1,0:T(8,128)(2,1)} %param.5) | copy-start | bytes 1769476
  10.6 110.0 %all-gather.5.cloned.1.call-start = ((), (), s32[]{:S(2)}) async-start(), calls=%async_computation.3 | async-start | bytes 2949120 | tf_op jit(solution)/shard_map/all_gather | solution.py:72
  10.7 33.6 %collective-permute-start = (bf16[256,1152]{1,0:T(8,128)(2,1)}, bf16[256,1152]{1,0:T(8,128)(2,1)S(1)}, u32[]{:S(2)}, u32[]{:S(2)}) collective-permute-start(bf16[256,1152]{1,0:T(8,128)(2,1)} %fusion.13), channel_id=1, source_target_pairs={{0,4},{4,8},{8,12},{12,16},{16,20},{20,24},{24,28},{28,32},{32,36}... | collective-permute-start | bytes 1769480 | tf_op jit(solution)/shard_map/ppermute | solution.py:11
  44.3 0.8 copy-start.1
  45.1 146.3 %reduce-scatter.3.cloned.1.call-start = ((), (), s32[]{:S(2)}) async-start(), calls=%async_computation.4 | async-start | bytes 2949120 | tf_op jit(solution)/shard_map/reduce_scatter | solution.py:89
  72.9 47.7 %copy-start.4 = (f32[256,1024]{1,0:T(8,128)}, f32[256,1024]{1,0:T(8,128)S(1)}, u32[]{:S(2)}) copy-start(f32[256,1024]{1,0:T(8,128)S(1)} %fusion.7) | copy-start | bytes 3145732
  75.6 187.4 %reduce-scatter.5.cloned.1.call-start = ((), (), s32[]{:S(2)}) async-start(), calls=%async_computation.5 | async-start | bytes 2949120 | tf_op jit(solution)/shard_map/reduce_scatter | solution.py:89
  124.6 1.0 copy-start.5
  128.2 1.7 copy-start.2
  129.8 2.3 copy-start.3
  129.8 2.4 copy-start.6
  191.5 71.5 %collective-permute-start.1 = (bf16[256,1152]{1,0:T(8,128)(2,1)}, bf16[256,1152]{1,0:T(8,128)(2,1)S(1)}, u32[]{:S(2)}, u32[]{:S(2)}) collective-permute-start(bf16[256,1152]{1,0:T(8,128)(2,1)} %reduce-scatter.3.cloned.1.call-done), channel_id=1, source_target_pairs={{0,4},{4,8},{8,12},{12,16},{16,20},{20,24},{24,28},{28,32},{32,36}... | collective-permute-start | bytes 1769480 | tf_op jit(solution)/shard_map/ppermute | solution.py:11
Sparse Core Ops, SparseCore 0:
  11.0 59.3 all-gather.2
  72.8 47.8 all-gather.4
  124.0 67.4 reduce-scatter.2
  195.1 67.8 reduce-scatter.4
where the time goes:
time: 272 us
  waiting for transfers between devices  223 us (82%)
  between operations  15.2 us (6%)
  matrix products  15.1 us (6%)
  other arithmetic  7.47 us (3%)
  starting transfers between devices  6.02 us (2%)
  local copies, waits for them, and re-layouts  4.2 us (2%)
    reduce_scatter x2, waiting for transfers between devices, local(): lax.psum_scatter(accumulated_cost_share.astype(jnp.bfloat16), 'grp', scat...  126 us
    all_gather x2, waiting for transfers between devices, local(): gathered_text = lax.all_gather(carried, 'grp', axis=0, tiled=True)  67.8 us
    ppermute x2, waiting for transfers between devices, from_behind(): lax.ppermute(value, axis, [(i, (i + by) % devices) for i in range(devices)])  29.7 us
    dot_general x2, matrix products, pairwise_terms(): lax.dot_general(picture_segment_entries, caption_segment_entries, (((1,),...  6.49 us
    ppermute x2, starting transfers between devices, from_behind(): lax.ppermute(value, axis, [(i, (i + by) % devices) for i in range(devices)])  5.86 us
  transfers between devices with their start and end apart: 6, of which 5 were waited for; matrix products, arithmetic and copies ran while one was open for 7% of the time, Pallas kernels for 0%

commit v1 on v0

v1 whole, which is shorter than its diff:
```python
import functools

import jax
import jax.numpy as jnp
from jax import lax
from jax.experimental import pallas as pl
from jax.experimental.pallas import tpu as pltpu
from jax.sharding import PartitionSpec as P

MESH = pl.DeviceIdType.MESH
STEPS = 2
ROWS = 256
CHUNK = 64
CHUNKS = ROWS // CHUNK
WIDE = 128
PLANE = 48
RELAYS = 16
RELAY_PLACE = 28
PIECE = ROWS // RELAYS
HELD = 2
EPS = 1e-06


def kernel(
    features,
    sharp_ref,
    bias_ref,
    weights_hbm,
    images_hbm,
    texts_hbm,
    image_grad_ref,
    text_grad_ref,
    row_loss_ref,
    images_ref,
    texts_ref,
    weight_ref,
    near,
    far,
    text,
    grads_near,
    grads_far,
    inverse,
    own_dir,
    near_out,
    near_in,
    far_out,
    far_in,
    back_out,
    back_in,
    carry_out,
    carry_in,
    relay,
    loss_out,
    loss_in,
    far_loss,
    text_sum,
    s_near,
    s_far,
    s_text,
    s_fwd,
    s_ndir,
    s_fdir,
    s_back,
    s_carry,
    s_loss,
    s_relay,
    s_load,
):
    loads = [
        pltpu.make_async_copy(
            images_hbm.at[pl.ds(0, CHUNK)], images_ref.at[pl.ds(0, CHUNK)], s_load.at[0]
        ),
        pltpu.make_async_copy(texts_hbm, texts_ref, s_load.at[1]),
        pltpu.make_async_copy(
            images_hbm.at[pl.ds(CHUNK, ROWS - CHUNK)],
            images_ref.at[pl.ds(CHUNK, ROWS - CHUNK)],
            s_load.at[2],
        ),
        pltpu.make_async_copy(weights_hbm, weight_ref, s_load.at[3]),
    ]
    for one in loads:
        one.start()
    blk = lax.axis_index("blk")
    member = lax.axis_index("grp")
    groups = lax.axis_size("blk")
    sibling = member + 1 - 2 * lax.rem(member, 2)
    opposite = lax.rem(member + 2, 4)
    diagonal = lax.rem(sibling + 2, 4)
    at_grp = lambda g: {"blk": blk, "grp": g}
    at_blk = lambda b: {"blk": b, "grp": member}
    ahead = lax.rem(blk + 1, groups)
    behind = lax.rem(blk + groups - 1, groups)
    place = lax.rem(blk, PLANE)
    base = blk - place
    next_base = lax.rem(base + PLANE, groups)
    last_base = lax.rem(base + groups - PLANE, groups)
    is_last = place == PLANE - 1
    is_first = place == 0
    piece = place - RELAY_PLACE
    is_relay = (piece >= 0) & (piece < RELAYS)
    relay_place = lambda j: RELAY_PLACE + j

    def copy(src, dst, sems, k, device):
        return pltpu.make_async_remote_copy(
            src_ref=src,
            dst_ref=dst,
            send_sem=sems.at[0, k],
            recv_sem=sems.at[1, k],
            device_id=device,
            device_id_type=MESH,
        )

    barrier = pltpu.get_barrier_semaphore()

    def greet(device):
        pl.semaphore_signal(barrier, inc=1, device_id=device, device_id_type=MESH)

    for other in (sibling, opposite, diagonal):
        greet(at_grp(other))

    @pl.when(is_first)
    def _():
        for j in range(RELAYS):
            greet(at_blk(base + relay_place(j)))

    @pl.when(jnp.logical_not(is_first))
    def _():
        greet(at_blk(behind))

    @pl.when(is_relay)
    def _():
        greet(at_blk(base + PLANE - 1))
        greet(at_blk(last_base + place))

    near_copy = copy(near.at[pl.ds(0, ROWS)], near.at[pl.ds(ROWS, ROWS)], s_near, 0, at_grp(sibling))

    def far_copy(c):
        return copy(
            near.at[pl.ds(c * CHUNK, CHUNK)],
            far.at[pl.ds(c * WIDE, CHUNK)],
            s_far,
            c,
            at_grp(opposite),
        )

    def forward_copy(c):
        return copy(
            far.at[pl.ds(c * WIDE, CHUNK)],
            far.at[pl.ds(c * WIDE + CHUNK, CHUNK)],
            s_fwd,
            c,
            at_grp(sibling),
        )

    def far_dir_copy(c):
        rows = pl.ds(c * CHUNK, CHUNK)
        return copy(far_out.at[rows], far_in.at[rows], s_fdir, c, at_grp(sibling))

    def back_copy(c):
        rows = pl.ds(c * CHUNK, CHUNK)
        return copy(back_out.at[rows], back_in.at[rows], s_back, c, at_grp(opposite))

    def pass_on(src, dst, start, sems):
        whole = copy(
            src.at[pl.ds(0, ROWS)], dst.at[pl.ds(start, ROWS)], sems, 0, at_blk(ahead)
        )

        @pl.when(is_last)
        def _():
            slot = relay.at[0] if sems is s_text else relay.at[2]
            for j in range(RELAYS):
                pltpu.make_async_remote_copy(
                    src_ref=src.at[pl.ds(j * PIECE, PIECE)],
                    dst_ref=slot,
                    send_sem=sems.at[0, 0],
                    recv_sem=s_relay.at[1, 0 if sems is s_text else 2],
                    device_id=at_blk(base + relay_place(j)),
                    device_id_type=MESH,
                ).start()

        @pl.when(jnp.logical_not(is_last))
        def _():
            whole.start()

        return whole

    def relay_hop(k):
        return pltpu.make_async_remote_copy(
            src_ref=relay.at[k],
            dst_ref=relay.at[k + 1],
            send_sem=s_relay.at[0, k],
            recv_sem=s_relay.at[1, k + 1],
            device_id=at_blk(next_base + place),
            device_id_type=MESH,
        )

    def relay_drop(k, dst, start, sems):
        return pltpu.make_async_remote_copy(
            src_ref=relay.at[k + 1],
            dst_ref=dst.at[pl.ds(pl.multiple_of(start + piece * PIECE, PIECE), PIECE)],
            send_sem=s_relay.at[0, k + 1],
            recv_sem=sems.at[1, 0],
            device_id=at_blk(base),
            device_id_type=MESH,
        )

    def relay_first(k):
        @pl.when(is_relay)
        def _():
            copy(relay.at[k], relay.at[k], s_relay, k, at_blk(ahead)).wait_recv()
            relay_hop(k).start()

    def relay_second(k, dst, start, sems):
        @pl.when(is_relay)
        def _():
            copy(relay.at[k], relay.at[k + 1], s_relay, k + 1, at_blk(ahead)).wait_recv()
            relay_drop(k, dst, start, sems).start()

    def unit(values):
        scale = lax.rsqrt(jnp.sum(values * values, axis=-1, keepdims=True) + EPS)
        return values * scale, scale

    def image_rows(c):
        rows = pl.ds(c * CHUNK, CHUNK)
        normed, scale = unit(images_ref[rows, :].astype(jnp.float32))
        near[rows, :] = normed.astype(jnp.bfloat16)
        inverse[rows, :] = jnp.broadcast_to(scale, (CHUNK, 128))

    def text_rows(c):
        rows = pl.ds(c * CHUNK, CHUNK)
        text[rows, :] = unit(texts_ref[rows, :].astype(jnp.float32))[0].astype(jnp.bfloat16)

    loads[0].wait()
    image_rows(0)
    loads[1].wait()
    for c in range(CHUNKS):
        text_rows(c)
    pl.semaphore_wait(barrier, jnp.where(is_last, 3 + RELAYS, jnp.where(is_relay, 6, 4)))
    far_copy(0).start()
    text_copy = pass_on(text, text, ROWS, s_text)
    loads[2].wait()
    for c in range(1, CHUNKS):
        image_rows(c)

        @pl.when(jnp.logical_not(is_relay))
        def _():
            far_copy(c).start()

    near_copy.start()
    loads[3].wait()

    sharp = jnp.exp(jnp.full((8, 128), sharp_ref[0], jnp.float32))
    sharp_row = sharp[0:1, :]
    bias = bias_ref[0]

    def pair_terms(products, weights, positive=None):
        logits = sharp_row * products + bias
        decay = jnp.exp(-jnp.abs(logits))
        share = jnp.where(logits >= 0, 1.0, decay) / (1.0 + decay)
        signed = logits
        if positive is not None:
            signed = jnp.where(positive, -logits, logits)
            share = jnp.where(positive, share - 1.0, share)
        losses = jnp.maximum(signed, 0.0) + jnp.log1p(decay)
        return jnp.sum(losses, axis=0, keepdims=True), (weights * share).astype(jnp.bfloat16)

    def against(some_text, some_images):
        return lax.dot_general(
            some_text, some_images, (((1,), (1,)), ((), ())), preferred_element_type=jnp.float32
        )

    def toward(some_grads, some_text):
        return lax.dot_general(
            some_grads, some_text, (((0,), (0,)), ((), ())), preferred_element_type=jnp.float32
        )

    def near_step(k, visit):
        slot, half = k // 2, k % 2
        owner = member if slot == 0 else sibling
        rows = pl.ds(k * WIDE, WIDE)
        texts_at = pl.ds(visit * ROWS, ROWS)
        weights = weight_ref[pl.ds(2 * owner + half, 1), :]
        positive = None
        if visit == 0 and slot == 0:
            shape = (ROWS, WIDE)
            positive = lax.broadcasted_iota(jnp.int32, shape, 0) == (
                lax.broadcasted_iota(jnp.int32, shape, 1) + half * WIDE
            )
        losses, grads = pair_terms(against(text[texts_at, :], near[rows, :]), weights, positive)
        grads_near[texts_at, rows] = grads
        if visit == 0:
            loss_out[slot, pl.ds(half, 1), :] = losses
        else:
            loss_out[slot, pl.ds(half, 1), :] += losses

    def near_dir(k):
        slot, half = k // 2, k % 2
        total = toward(grads_near[:, pl.ds(k * WIDE, WIDE)], text[...])
        rows = pl.ds(half * WIDE, WIDE)
        if slot == 0:
            own_dir[rows, :] = total
        else:
            near_out[rows, :] = total.astype(jnp.bfloat16)

    left = lax.broadcasted_iota(jnp.int32, (1, WIDE), 1) < CHUNK
    swap = lambda row: pltpu.roll(row, CHUNK, 1)

    def far_step(c, visits):
        rows = pl.ds(c * WIDE, WIDE)
        texts_at = pl.ds(visits[0] * ROWS, len(visits) * ROWS)
        one = weight_ref[pl.ds(2 * opposite + c // 2, 1), :]
        two = weight_ref[pl.ds(2 * diagonal + c // 2, 1), :]
        weights = jnp.where(left, one, swap(two)) if c % 2 == 0 else jnp.where(left, swap(one), two)
        losses, grads = pair_terms(against(text[texts_at, :], far[rows, :]), weights)
        grads_far[texts_at, rows] = grads
        if visits[0] == 0:
            far_loss[c, pl.ds(0, 1), :] = losses
        else:
            far_loss[c, pl.ds(0, 1), :] += losses

    def far_dir(c):
        total = toward(grads_far[:, pl.ds(c * WIDE, WIDE)], text[...])
        far_out[pl.ds(c * CHUNK, CHUNK), :] = total[CHUNK:].astype(jnp.bfloat16)
        far_dir_copy(c).start()
        return total[:CHUNK]

    def far_arrives(c):
        far_copy(c).wait_recv()
        forward_copy(c).start()
        forward_copy(c).wait_recv()

    def far_sum(c, mine):
        far_dir_copy(c).wait_recv()
        rows = pl.ds(c * CHUNK, CHUNK)
        back_out[rows, :] = (mine + far_in[rows, :].astype(jnp.float32)).astype(jnp.bfloat16)

    def text_near(visit):
        texts_at = pl.ds(visit * ROWS, ROWS)
        text_sum[texts_at, :] = jnp.dot(
            grads_near[texts_at, :], near[...], preferred_element_type=jnp.float32
        )

    def text_total(visit):
        texts_at = pl.ds(visit * ROWS, ROWS)
        return sharp[0:1, 0:1] * (
            text_sum[texts_at, :]
            + jnp.dot(grads_far[texts_at, :], far[...], preferred_element_type=jnp.float32)
        )

    near_step(0, 0)
    relay_first(0)

    @pl.when(is_relay)
    def _():
        for c in range(1, CHUNKS):
            far_copy(c).start()

    near_step(1, 0)
    near_copy.wait_recv()
    relay_second(0, text, ROWS, s_text)
    near_step(2, 0)
    near_step(3, 0)

    near_dir_copy = copy(near_out, near_in, s_ndir, 0, at_grp(sibling))
    for c in range(CHUNKS):
        far_arrives(c)
        if c == 0:
            far_step(c, (0,))
            text_near(0)
            text_copy.wait_recv()
            far_step(c, (1,))
        else:
            far_step(c, (0, 1))
        mine = far_dir(c)
        if c == 0:
            near_step(0, 1)
            near_step(1, 1)
        if c == 1:
            near_step(2, 1)
            near_step(3, 1)
        if c == 2:
            near_dir(2)
            near_dir(3)
            near_dir_copy.start()
        far_sum(c, mine)
        if c < HELD:
            back_copy(c).start()
        else:

            @pl.when(jnp.logical_not(is_relay))
            def _():
                back_copy(c).start()

    carry_out[...] = text_total(0).astype(jnp.bfloat16)
    carry_copy = pass_on(carry_out, carry_in, 0, s_carry)
    near_dir(0)
    near_dir(1)
    text_near(1)

    for half in range(2):
        even, odd = far_loss[2 * half, 0:1, :], far_loss[2 * half + 1, 0:1, :]
        loss_out[2, pl.ds(half, 1), :] = jnp.where(left, even, swap(odd))
        loss_out[3, pl.ds(half, 1), :] = jnp.where(left, swap(even), odd)
    loss_copies = [
        copy(loss_out.at[k + 1], loss_in.at[k], s_loss, k, at_grp(other))
        for k, other in enumerate((sibling, opposite, diagonal))
    ]
    for one in loss_copies:
        one.start()

    relay_first(2)

    @pl.when(is_relay)
    def _():
        for c in range(HELD, CHUNKS):
            back_copy(c).start()

    text_sum[pl.ds(ROWS, ROWS), :] = text_total(1)
    relay_second(2, carry_in, 0, s_carry)
    carry_copy.wait_recv()
    text_grad_ref[...] = (text_sum[pl.ds(ROWS, ROWS), :] + carry_in[...].astype(jnp.float32)).astype(
        jnp.bfloat16
    )

    for one in loss_copies:
        one.wait_recv()
    total_loss = loss_out[0] + loss_in[0] + loss_in[1] + loss_in[2]
    row_loss_ref[...] = total_loss[0:2, :] / (STEPS * 4 * ROWS)

    near_dir_copy.wait_recv()
    for c in range(CHUNKS):
        rows = pl.ds(c * CHUNK, CHUNK)
        back_copy(c).wait_recv()
        step = sharp[0:1, 0:1] * (
            own_dir[rows, :]
            + near_in[rows, :].astype(jnp.float32)
            + back_in[rows, :].astype(jnp.float32)
        )
        scale = inverse[rows, 0:1]
        normed = images_ref[rows, :].astype(jnp.float32) * scale
        image_grad_ref[rows, :] = scale * (
            step - normed * jnp.sum(normed * step, axis=-1, keepdims=True)
        )

    near_copy.wait_send()
    text_copy.wait_send()
    near_dir_copy.wait_send()
    carry_copy.wait_send()
    for one in loss_copies:
        one.wait_send()
    for c in range(CHUNKS):
        far_copy(c).wait_send()
        forward_copy(c).wait_send()
        far_dir_copy(c).wait_send()
        back_copy(c).wait_send()

    @pl.when(is_relay)
    def _():
        for k, dst, start, sems in ((0, text, ROWS, s_text), (2, carry_in, 0, s_carry)):
            relay_hop(k).wait_send()
            relay_drop(k, dst, start, sems).wait_send()


def local(images, texts, row_weight, log_sharpness_parameter, bias):
    rows, features = images.shape
    vmem = pl.BlockSpec(memory_space=pltpu.VMEM)
    smem = pl.BlockSpec(memory_space=pltpu.SMEM)
    hbm = pl.BlockSpec(memory_space=pltpu.HBM)
    half = lambda n: pltpu.VMEM((n, features), jnp.bfloat16)
    sems = lambda n: pltpu.SemaphoreType.DMA((2, n))
    image_grad, text_grad, row_loss = pl.pallas_call(
        functools.partial(kernel, features),
        out_shape=(
            jax.ShapeDtypeStruct((rows, features), jnp.float32),
            jax.ShapeDtypeStruct((rows, features), jnp.bfloat16),
            jax.ShapeDtypeStruct((2, 128), jnp.float32),
        ),
        in_specs=[smem, smem, hbm, hbm, hbm],
        out_specs=(vmem, vmem, vmem),
        scratch_shapes=[
            half(ROWS),
            half(ROWS),
            pltpu.VMEM((8, 128), jnp.float32),
            half(2 * ROWS),
            half(2 * ROWS),
            half(2 * ROWS),
            pltpu.VMEM((2 * ROWS, 2 * ROWS), jnp.bfloat16),
            pltpu.VMEM((2 * ROWS, 2 * ROWS), jnp.bfloat16),
            pltpu.VMEM((ROWS, 128), jnp.float32),
            pltpu.VMEM((ROWS, features), jnp.float32),
            half(ROWS),
            half(ROWS),
            half(ROWS),
            half(ROWS),
            half(ROWS),
            half(ROWS),
            half(ROWS),
            half(ROWS),
            pltpu.VMEM((4, PIECE, features), jnp.bfloat16),
            pltpu.VMEM((4, 8, 128), jnp.float32),
            pltpu.VMEM((3, 8, 128), jnp.float32),
            pltpu.VMEM((CHUNKS, 8, 128), jnp.float32),
            pltpu.VMEM((2 * ROWS, features), jnp.float32),
            sems(1),
            sems(CHUNKS),
            sems(1),
            sems(CHUNKS),
            sems(1),
            sems(CHUNKS),
            sems(CHUNKS),
            sems(1),
            sems(3),
            sems(4),
            pltpu.SemaphoreType.DMA((4,)),
        ],
        compiler_params=pltpu.CompilerParams(
            collective_id=0, has_side_effects=True, vmem_limit_bytes=48 << 20
        ),
        name="pairs",
    )(log_sharpness_parameter, bias, row_weight.reshape(8, 128), images, texts)
    return (image_grad, text_grad, row_loss.reshape(rows))


def solution(mesh):
    placed = (P(("blk", "grp"), None), P(("blk", "grp"), None), P("blk"), P(), P())
    return jax.shard_map(
        local,
        mesh=mesh,
        in_specs=placed,
        out_specs=(P(("blk", "grp"), None), P(("blk", "grp"), None), P(("blk", "grp"))),
        check_vma=False,
    )
```

time: 272 us -> 97.8 us (0.36)
  the two profiles are of different devices: /device:TPU:1 before, /device:TPU:48 now
where the time goes in v1:
time: 97.8 us; the launch traced here: 97.5 us
  Pallas kernels  90.3 us (92%)
  local copies, waits for them, and re-layouts  5.2 us (5%)
  between operations  1.94 us (2%)
    pallas_call x1, Pallas kernels, local(): pl.pallas_call(functools.partial(kernel, features), out_shape=(jax.ShapeD...  90.3 us
    unnamed x9, local copies, waits for them, and re-layouts  5.2 us

profile of v1, /device:TPU:48, one launch (start us, length us, event | category | flops | bytes accessed | tf_op | source)
XLA Modules:
  0.0 97.5 jit_solution(14743716898489851906)
XLA Ops:
  1.9 0.0 copy-start
  1.9 1.1 %copy-done = bf16[256,1152]{1,0:T(8,128)(2,1)S(1)} copy-done((bf16[256,1152]{1,0:T(8,128)(2,1)S(1)}, bf16[256,1152]{1,0:T(8,128)(2,1)}, u32[]{:S(2)}) %copy-start) | copy-done | bytes 589848
  3.0 0.0 copy-start.1
  3.0 1.1 %copy-done.1 = bf16[256,1152]{1,0:T(8,128)(2,1)S(1)} copy-done((bf16[256,1152]{1,0:T(8,128)(2,1)S(1)}, bf16[256,1152]{1,0:T(8,128)(2,1)}, u32[]{:S(2)}) %copy-start.1) | copy-done | bytes 589848
  4.1 0.0 copy-start.2
  4.1 0.7 copy-done.2
  4.7 90.3 %pairs.1 = (f32[256,1152]{1,0:T(8,128)S(1)}, bf16[256,1152]{1,0:T(8,128)(2,1)S(1)}, f32[2,128]{1,0:T(2,128)S(1)}) custom-call(f32[1]{0:T(128)S(6)} %copy.11.sharp_ref, f32[1]{0:T(128)S(6)} %copy.12.bias_ref, f32[8,128]{1,0:T(8,128)S(1)} %bitcast.2, bf16[256,1152]{1,0:T(8,128)(2,1)S(1)} %copy-done, bf16[256,1152]{1,0:T(8,128)(2,1)S(1)} %copy-done.1), custom_call_target="tpu_custom_call" | custom-call | tf_op jit(solution)/shard_map/pairs/pallas_call | solution.py:471
  95.1 1.0 %copy.13 = f32[256,1152]{1,0:T(8,128)} copy(f32[256,1152]{1,0:T(8,128)S(1)} %get-tuple-element.12) | data formatting | bytes 2359296
  96.1 0.8 copy.14
  96.9 0.6 copy.15
Async XLA Ops:
  1.9 1.1 %copy-start = (bf16[256,1152]{1,0:T(8,128)(2,1)S(1)}, bf16[256,1152]{1,0:T(8,128)(2,1)}, u32[]{:S(2)}) copy-start(bf16[256,1152]{1,0:T(8,128)(2,1)} %images_hbm.1) | copy-start | bytes 1769476
  3.0 1.1 %copy-start.1 = (bf16[256,1152]{1,0:T(8,128)(2,1)S(1)}, bf16[256,1152]{1,0:T(8,128)(2,1)}, u32[]{:S(2)}) copy-start(bf16[256,1152]{1,0:T(8,128)(2,1)} %texts_hbm.1) | copy-start | bytes 1769476
  4.1 0.7 copy-start.2

commit v2 on v1

--- a/solution.py
+++ b/solution.py
@@ -14,10 +14,8 @@
 CHUNKS = ROWS // CHUNK
 WIDE = 128
 PLANE = 48
-RELAYS = 16
-RELAY_PLACE = 28
-PIECE = ROWS // RELAYS
-HELD = 2
+RELAYS = ((44, True), (45, True), (46, True)) + tuple((p, False) for p in (40, 36, 33, 4, 3))
+PIECE = ROWS // len(RELAYS)
 EPS = 1e-06
 
 
@@ -96,9 +94,9 @@
     last_base = lax.rem(base + groups - PLANE, groups)
     is_last = place == PLANE - 1
     is_first = place == 0
-    piece = place - RELAY_PLACE
-    is_relay = (piece >= 0) & (piece < RELAYS)
-    relay_place = lambda j: RELAY_PLACE + j
+    is_relay = functools.reduce(jnp.logical_or, [place == p for p, _ in RELAYS])
+    piece = sum(j * (place == p).astype(jnp.int32) for j, (p, _) in enumerate(RELAYS))
+    at_old = functools.reduce(jnp.logical_or, [place == p for p, old in RELAYS if old])
 
     def copy(src, dst, sems, k, device):
         return pltpu.make_async_remote_copy(
@@ -120,8 +118,8 @@
 
     @pl.when(is_first)
     def _():
-        for j in range(RELAYS):
-            greet(at_blk(base + relay_place(j)))
+        for p, old in RELAYS:
+            greet(at_blk((last_base if old else base) + p))
 
     @pl.when(jnp.logical_not(is_first))
     def _():
@@ -129,8 +127,7 @@
 
     @pl.when(is_relay)
     def _():
-        greet(at_blk(base + PLANE - 1))
-        greet(at_blk(last_base + place))
+        greet(at_blk(jnp.where(at_old, base, last_base) + PLANE - 1))
 
     near_copy = copy(near.at[pl.ds(0, ROWS)], near.at[pl.ds(ROWS, ROWS)], s_near, 0, at_grp(sibling))
 
@@ -167,14 +164,14 @@
 
         @pl.when(is_last)
         def _():
-            slot = relay.at[0] if sems is s_text else relay.at[2]
-            for j in range(RELAYS):
+            k = 0 if sems is s_text else 1
+            for j, (p, old) in enumerate(RELAYS):
                 pltpu.make_async_remote_copy(
                     src_ref=src.at[pl.ds(j * PIECE, PIECE)],
-                    dst_ref=slot,
+                    dst_ref=relay.at[k],
                     send_sem=sems.at[0, 0],
-                    recv_sem=s_relay.at[1, 0 if sems is s_text else 2],
-                    device_id=at_blk(base + relay_place(j)),
+                    recv_sem=s_relay.at[1, k],
+                    device_id=at_blk((base if old else next_base) + p),
                     device_id_type=MESH,
                 ).start()
 
@@ -184,37 +181,21 @@
 
         return whole
 
-    def relay_hop(k):
+    def relay_copy(k, dst, start, sems):
         return pltpu.make_async_remote_copy(
             src_ref=relay.at[k],
-            dst_ref=relay.at[k + 1],
+            dst_ref=dst.at[pl.ds(pl.multiple_of(start + piece * PIECE, PIECE), PIECE)],
             send_sem=s_relay.at[0, k],
-            recv_sem=s_relay.at[1, k + 1],
-            device_id=at_blk(next_base + place),
+            recv_sem=sems.at[1, 0],
+            device_id=at_blk(jnp.where(at_old, next_base, base)),
             device_id_type=MESH,
         )
 
-    def relay_drop(k, dst, start, sems):
-        return pltpu.make_async_remote_copy(
-            src_ref=relay.at[k + 1],
-            dst_ref=dst.at[pl.ds(pl.multiple_of(start + piece * PIECE, PIECE), PIECE)],
-            send_sem=s_relay.at[0, k + 1],
-            recv_sem=sems.at[1, 0],
-            device_id=at_blk(base),
-            device_id_type=MESH,
-        )
-
-    def relay_first(k):
+    def relay_on(k, dst, start, sems):
         @pl.when(is_relay)
         def _():
             copy(relay.at[k], relay.at[k], s_relay, k, at_blk(ahead)).wait_recv()
-            relay_hop(k).start()
-
-    def relay_second(k, dst, start, sems):
-        @pl.when(is_relay)
-        def _():
-            copy(relay.at[k], relay.at[k + 1], s_relay, k + 1, at_blk(ahead)).wait_recv()
-            relay_drop(k, dst, start, sems).start()
+            relay_copy(k, dst, start, sems).start()
 
     def unit(values):
         scale = lax.rsqrt(jnp.sum(values * values, axis=-1, keepdims=True) + EPS)
@@ -235,16 +216,13 @@
     loads[1].wait()
     for c in range(CHUNKS):
         text_rows(c)
-    pl.semaphore_wait(barrier, jnp.where(is_last, 3 + RELAYS, jnp.where(is_relay, 6, 4)))
+    pl.semaphore_wait(barrier, jnp.where(is_last, 3 + len(RELAYS), jnp.where(is_relay, 5, 4)))
     far_copy(0).start()
     text_copy = pass_on(text, text, ROWS, s_text)
     loads[2].wait()
     for c in range(1, CHUNKS):
         image_rows(c)
-
-        @pl.when(jnp.logical_not(is_relay))
-        def _():
-            far_copy(c).start()
+        far_copy(c).start()
 
     near_copy.start()
     loads[3].wait()
@@ -305,15 +283,15 @@
     left = lax.broadcasted_iota(jnp.int32, (1, WIDE), 1) < CHUNK
     swap = lambda row: pltpu.roll(row, CHUNK, 1)
 
-    def far_step(c, visits):
+    def far_step(c, visit):
         rows = pl.ds(c * WIDE, WIDE)
-        texts_at = pl.ds(visits[0] * ROWS, len(visits) * ROWS)
+        texts_at = pl.ds(visit * ROWS, ROWS)
         one = weight_ref[pl.ds(2 * opposite + c // 2, 1), :]
         two = weight_ref[pl.ds(2 * diagonal + c // 2, 1), :]
         weights = jnp.where(left, one, swap(two)) if c % 2 == 0 else jnp.where(left, swap(one), two)
         losses, grads = pair_terms(against(text[texts_at, :], far[rows, :]), weights)
         grads_far[texts_at, rows] = grads
-        if visits[0] == 0:
+        if visit == 0:
             far_loss[c, pl.ds(0, 1), :] = losses
         else:
             far_loss[c, pl.ds(0, 1), :] += losses
@@ -348,53 +326,50 @@
         )
 
     near_step(0, 0)
-    relay_first(0)
-
-    @pl.when(is_relay)
-    def _():
-        for c in range(1, CHUNKS):
-            far_copy(c).start()
-
     near_step(1, 0)
     near_copy.wait_recv()
-    relay_second(0, text, ROWS, s_text)
     near_step(2, 0)
     near_step(3, 0)
+    relay_on(0, text, ROWS, s_text)
 
     near_dir_copy = copy(near_out, near_in, s_ndir, 0, at_grp(sibling))
+    for c in range(2):
+        far_arrives(c)
+        far_step(c, 0)
+    text_near(0)
+
+    @pl.when(is_first)
+    def _():
+        for c in range(2, CHUNKS):
+            far_arrives(c)
+            far_step(c, 0)
+
+    text_copy.wait_recv()
     for c in range(CHUNKS):
-        far_arrives(c)
-        if c == 0:
-            far_step(c, (0,))
-            text_near(0)
-            text_copy.wait_recv()
-            far_step(c, (1,))
-        else:
-            far_step(c, (0, 1))
+        if c >= 2:
+
+            @pl.when(jnp.logical_not(is_first))
+            def _():
+                far_arrives(c)
+                far_step(c, 0)
+
+        far_step(c, 1)
         mine = far_dir(c)
-        if c == 0:
-            near_step(0, 1)
-            near_step(1, 1)
-        if c == 1:
-            near_step(2, 1)
-            near_step(3, 1)
+        if c < 2:
+            near_step(2 * c, 1)
+            near_step(2 * c + 1, 1)
         if c == 2:
             near_dir(2)
             near_dir(3)
             near_dir_copy.start()
+        if c == 3:
+            near_dir(0)
+            near_dir(1)
         far_sum(c, mine)
-        if c < HELD:
-            back_copy(c).start()
-        else:
-
-            @pl.when(jnp.logical_not(is_relay))
-            def _():
-                back_copy(c).start()
+        back_copy(c).start()
 
     carry_out[...] = text_total(0).astype(jnp.bfloat16)
     carry_copy = pass_on(carry_out, carry_in, 0, s_carry)
-    near_dir(0)
-    near_dir(1)
     text_near(1)
 
     for half in range(2):
@@ -408,15 +383,8 @@
     for one in loss_copies:
         one.start()
 
-    relay_first(2)
-
-    @pl.when(is_relay)
-    def _():
-        for c in range(HELD, CHUNKS):
-            back_copy(c).start()
-
     text_sum[pl.ds(ROWS, ROWS), :] = text_total(1)
-    relay_second(2, carry_in, 0, s_carry)
+    relay_on(1, carry_in, 0, s_carry)
     carry_copy.wait_recv()
     text_grad_ref[...] = (text_sum[pl.ds(ROWS, ROWS), :] + carry_in[...].astype(jnp.float32)).astype(
         jnp.bfloat16
@@ -456,9 +424,8 @@
 
     @pl.when(is_relay)
     def _():
-        for k, dst, start, sems in ((0, text, ROWS, s_text), (2, carry_in, 0, s_carry)):
-            relay_hop(k).wait_send()
-            relay_drop(k, dst, start, sems).wait_send()
+        relay_copy(0, text, ROWS, s_text).wait_send()
+        relay_copy(1, carry_in, 0, s_carry).wait_send()
 
 
 def local(images, texts, row_weight, log_sharpness_parameter, bias):
@@ -468,6 +435,10 @@
     hbm = pl.BlockSpec(memory_space=pltpu.HBM)
     half = lambda n: pltpu.VMEM((n, features), jnp.bfloat16)
     sems = lambda n: pltpu.SemaphoreType.DMA((2, n))
+    stay = [
+        pltpu.with_memory_space_constraint(value, pltpu.HBM)
+        for value in (row_weight.reshape(8, 128), images, texts)
+    ]
     image_grad, text_grad, row_loss = pl.pallas_call(
         functools.partial(kernel, features),
         out_shape=(
@@ -496,7 +467,7 @@
             half(ROWS),
             half(ROWS),
             half(ROWS),
-            pltpu.VMEM((4, PIECE, features), jnp.bfloat16),
+            pltpu.VMEM((2, PIECE, features), jnp.bfloat16),
             pltpu.VMEM((4, 8, 128), jnp.float32),
             pltpu.VMEM((3, 8, 128), jnp.float32),
             pltpu.VMEM((CHUNKS, 8, 128), jnp.float32),
@@ -510,14 +481,14 @@
             sems(CHUNKS),
             sems(1),
             sems(3),
-            sems(4),
+            sems(2),
             pltpu.SemaphoreType.DMA((4,)),
         ],
         compiler_params=pltpu.CompilerParams(
             collective_id=0, has_side_effects=True, vmem_limit_bytes=48 << 20
         ),
         name="pairs",
-    )(log_sharpness_parameter, bias, row_weight.reshape(8, 128), images, texts)
+    )(log_sharpness_parameter, bias, *stay)
     return (image_grad, text_grad, row_loss.reshape(rows))
 
 

time: 97.8 us -> 81.4 us (0.83)
  the two profiles are of different devices: /device:TPU:48 before, /device:TPU:1 now
where the time goes in v2:
time: 81.4 us; the launch traced here: 81.3 us
  Pallas kernels  76.9 us (94%)
  local copies, waits for them, and re-layouts  2.39 us (3%)
  between operations  1.93 us (2%)
    pallas_call x1, Pallas kernels, local(): pl.pallas_call(functools.partial(kernel, features), out_shape=(jax.ShapeD...  76.9 us
    unnamed x3, local copies, waits for them, and re-layouts  2.39 us

profile of v2, /device:TPU:1, one launch (start us, length us, event | category | flops | bytes accessed | tf_op | source)
XLA Modules:
  0.0 81.3 jit_solution(14136459520935749058)
XLA Ops:
  1.9 76.9 %pairs.1 = (f32[256,1152]{1,0:T(8,128)S(1)}, bf16[256,1152]{1,0:T(8,128)(2,1)S(1)}, f32[2,128]{1,0:T(2,128)S(1)}) custom-call(f32[1]{0:T(128)S(6)} %copy.11.sharp_ref, f32[1]{0:T(128)S(6)} %copy.12.bias_ref, f32[8,128]{1,0:T(8,128)} %bitcast.3, bf16[256,1152]{1,0:T(8,128)(2,1)} %images_hbm.1, bf16[256,1152]{1,0:T(8,128)(2,1)} %texts_hbm.1), custom_call_target="tpu_custom_call" | custom-call | tf_op jit(solution)/shard_map/pairs/pallas_call | solution.py:442
  78.9 1.0 %copy.13 = f32[256,1152]{1,0:T(8,128)} copy(f32[256,1152]{1,0:T(8,128)S(1)} %get-tuple-element.12) | data formatting | bytes 2359296
  79.9 0.8 %copy.14 = bf16[256,1152]{1,0:T(8,128)(2,1)} copy(bf16[256,1152]{1,0:T(8,128)(2,1)S(1)} %get-tuple-element.13) | data formatting | bytes 1179648
  80.7 0.6 copy.15

commit v3 on v2

--- a/solution.py
+++ b/solution.py
@@ -14,7 +14,7 @@
 CHUNKS = ROWS // CHUNK
 WIDE = 128
 PLANE = 48
-RELAYS = ((44, True), (45, True), (46, True)) + tuple((p, False) for p in (40, 36, 33, 4, 3))
+RELAYS = ((45, True), (46, True)) + tuple((p, False) for p in (40, 36, 33, 8, 4, 3))
 PIECE = ROWS // len(RELAYS)
 EPS = 1e-06
 
@@ -68,7 +68,7 @@
         pltpu.make_async_copy(
             images_hbm.at[pl.ds(0, CHUNK)], images_ref.at[pl.ds(0, CHUNK)], s_load.at[0]
         ),
-        pltpu.make_async_copy(texts_hbm, texts_ref, s_load.at[1]),
+        pltpu.make_async_copy(texts_hbm, texts_ref.at[pl.ds(0, ROWS)], s_load.at[1]),
         pltpu.make_async_copy(
             images_hbm.at[pl.ds(CHUNK, ROWS - CHUNK)],
             images_ref.at[pl.ds(CHUNK, ROWS - CHUNK)],
@@ -213,18 +213,18 @@
 
     loads[0].wait()
     image_rows(0)
-    loads[1].wait()
-    for c in range(CHUNKS):
-        text_rows(c)
     pl.semaphore_wait(barrier, jnp.where(is_last, 3 + len(RELAYS), jnp.where(is_relay, 5, 4)))
     far_copy(0).start()
-    text_copy = pass_on(text, text, ROWS, s_text)
+    text_copy = pass_on(texts_hbm, texts_ref, ROWS, s_text)
     loads[2].wait()
     for c in range(1, CHUNKS):
         image_rows(c)
         far_copy(c).start()
 
     near_copy.start()
+    loads[1].wait()
+    for c in range(CHUNKS):
+        text_rows(c)
     loads[3].wait()
 
     sharp = jnp.exp(jnp.full((8, 128), sharp_ref[0], jnp.float32))
@@ -318,19 +318,20 @@
             grads_near[texts_at, :], near[...], preferred_element_type=jnp.float32
         )
 
-    def text_total(visit):
+    def text_far(visit, rows):
         texts_at = pl.ds(visit * ROWS, ROWS)
-        return sharp[0:1, 0:1] * (
-            text_sum[texts_at, :]
-            + jnp.dot(grads_far[texts_at, :], far[...], preferred_element_type=jnp.float32)
-        )
+        return text_sum[texts_at, :] + jnp.dot(
+            grads_far[texts_at, rows], far[rows, :], preferred_element_type=jnp.float32
+        )
+
+    early, late = pl.ds(0, 3 * WIDE), pl.ds(3 * WIDE, WIDE)
 
     near_step(0, 0)
     near_step(1, 0)
     near_copy.wait_recv()
     near_step(2, 0)
     near_step(3, 0)
-    relay_on(0, text, ROWS, s_text)
+    relay_on(0, texts_ref, ROWS, s_text)
 
     near_dir_copy = copy(near_out, near_in, s_ndir, 0, at_grp(sibling))
     for c in range(2):
@@ -345,6 +346,8 @@
             far_step(c, 0)
 
     text_copy.wait_recv()
+    for c in range(CHUNKS, 2 * CHUNKS):
+        text_rows(c)
     for c in range(CHUNKS):
         if c >= 2:
 
@@ -353,6 +356,9 @@
                 far_arrives(c)
                 far_step(c, 0)
 
+        if c == CHUNKS - 1:
+            carry_out[...] = (sharp[0:1, 0:1] * text_far(0, late)).astype(jnp.bfloat16)
+            carry_copy = pass_on(carry_out, carry_in, 0, s_carry)
         far_step(c, 1)
         mine = far_dir(c)
         if c < 2:
@@ -362,15 +368,12 @@
             near_dir(2)
             near_dir(3)
             near_dir_copy.start()
+            text_sum[pl.ds(0, ROWS), :] = text_far(0, early)
         if c == 3:
             near_dir(0)
             near_dir(1)
         far_sum(c, mine)
         back_copy(c).start()
-
-    carry_out[...] = text_total(0).astype(jnp.bfloat16)
-    carry_copy = pass_on(carry_out, carry_in, 0, s_carry)
-    text_near(1)
 
     for half in range(2):
         even, odd = far_loss[2 * half, 0:1, :], far_loss[2 * half + 1, 0:1, :]
@@ -383,12 +386,9 @@
     for one in loss_copies:
         one.start()
 
-    text_sum[pl.ds(ROWS, ROWS), :] = text_total(1)
+    text_near(1)
+    text_sum[pl.ds(ROWS, ROWS), :] = sharp[0:1, 0:1] * text_far(1, pl.ds(0, 2 * ROWS))
     relay_on(1, carry_in, 0, s_carry)
-    carry_copy.wait_recv()
-    text_grad_ref[...] = (text_sum[pl.ds(ROWS, ROWS), :] + carry_in[...].astype(jnp.float32)).astype(
-        jnp.bfloat16
-    )
 
     for one in loss_copies:
         one.wait_recv()
@@ -398,6 +398,11 @@
     near_dir_copy.wait_recv()
     for c in range(CHUNKS):
         rows = pl.ds(c * CHUNK, CHUNK)
+        if c == CHUNKS - 1:
+            carry_copy.wait_recv()
+            text_grad_ref[...] = (
+                text_sum[pl.ds(ROWS, ROWS), :] + carry_in[...].astype(jnp.float32)
+            ).astype(jnp.bfloat16)
         back_copy(c).wait_recv()
         step = sharp[0:1, 0:1] * (
             own_dir[rows, :]
@@ -424,7 +429,7 @@
 
     @pl.when(is_relay)
     def _():
-        relay_copy(0, text, ROWS, s_text).wait_send()
+        relay_copy(0, texts_ref, ROWS, s_text).wait_send()
         relay_copy(1, carry_in, 0, s_carry).wait_send()
 
 
@@ -450,7 +455,7 @@
         out_specs=(vmem, vmem, vmem),
         scratch_shapes=[
             half(ROWS),
-            half(ROWS),
+            half(2 * ROWS),
             pltpu.VMEM((8, 128), jnp.float32),
             half(2 * ROWS),
             half(2 * ROWS),

time: 81.4 us -> 74.6 us (0.916)
  Pallas kernels: 76.9 us -> 70.1 us
    pallas_call x1, Pallas kernels: 76.9 us -> 70.1 us  [local(): pl.pallas_call(functools.partial(kernel, features), out_shape=(jax.ShapeD...]
where the time goes in v3:
time: 74.6 us; the launch traced here: 74.4 us
  Pallas kernels  70.1 us (94%)
  local copies, waits for them, and re-layouts  2.39 us (3%)
  between operations  1.93 us (3%)
    pallas_call x1, Pallas kernels, local(): pl.pallas_call(functools.partial(kernel, features), out_shape=(jax.ShapeD...  70.1 us
    unnamed x3, local copies, waits for them, and re-layouts  2.39 us

profile of v3, /device:TPU:1, one launch (start us, length us, event | category | flops | bytes accessed | tf_op | source)
XLA Modules:
  0.0 74.4 jit_solution(4702988256054406308)
XLA Ops:
  1.9 70.1 %pairs.1 = (f32[256,1152]{1,0:T(8,128)S(1)}, bf16[256,1152]{1,0:T(8,128)(2,1)S(1)}, f32[2,128]{1,0:T(2,128)S(1)}) custom-call(f32[1]{0:T(128)S(6)} %copy.11.sharp_ref, f32[1]{0:T(128)S(6)} %copy.12.bias_ref, f32[8,128]{1,0:T(8,128)} %bitcast.3, bf16[256,1152]{1,0:T(8,128)(2,1)} %images_hbm.1, bf16[256,1152]{1,0:T(8,128)(2,1)} %texts_hbm.1), custom_call_target="tpu_custom_call" | custom-call | tf_op jit(solution)/shard_map/pairs/pallas_call | solution.py:447
  72.1 1.0 %copy.13 = f32[256,1152]{1,0:T(8,128)} copy(f32[256,1152]{1,0:T(8,128)S(1)} %get-tuple-element.12) | data formatting | bytes 2359296
  73.1 0.8 %copy.14 = bf16[256,1152]{1,0:T(8,128)(2,1)} copy(bf16[256,1152]{1,0:T(8,128)(2,1)S(1)} %get-tuple-element.13) | data formatting | bytes 1179648
  73.9 0.6 copy.15

commit v4 on v3

--- a/solution.py
+++ b/solution.py
@@ -339,23 +339,13 @@
         far_step(c, 0)
     text_near(0)
 
-    @pl.when(is_first)
-    def _():
-        for c in range(2, CHUNKS):
-            far_arrives(c)
-            far_step(c, 0)
-
     text_copy.wait_recv()
     for c in range(CHUNKS, 2 * CHUNKS):
         text_rows(c)
     for c in range(CHUNKS):
         if c >= 2:
-
-            @pl.when(jnp.logical_not(is_first))
-            def _():
-                far_arrives(c)
-                far_step(c, 0)
-
+            far_arrives(c)
+            far_step(c, 0)
         if c == CHUNKS - 1:
             carry_out[...] = (sharp[0:1, 0:1] * text_far(0, late)).astype(jnp.bfloat16)
             carry_copy = pass_on(carry_out, carry_in, 0, s_carry)

time: 74.6 us -> 74.4 us (level)
  no operation moved by 1% of the time
where the time goes in v4:
time: 74.4 us; the launch traced here: 74.2 us
  Pallas kernels  69.9 us (94%)
  local copies, waits for them, and re-layouts  2.39 us (3%)
  between operations  1.93 us (3%)
    pallas_call x1, Pallas kernels, local(): pl.pallas_call(functools.partial(kernel, features), out_shape=(jax.ShapeD...  69.9 us
    unnamed x3, local copies, waits for them, and re-layouts  2.39 us

profile of v4, /device:TPU:1, one launch (start us, length us, event | category | flops | bytes accessed | tf_op | source)
XLA Modules:
  0.0 74.2 jit_solution(13556072013977400696)
XLA Ops:
  1.9 69.9 %pairs.1 = (f32[256,1152]{1,0:T(8,128)S(1)}, bf16[256,1152]{1,0:T(8,128)(2,1)S(1)}, f32[2,128]{1,0:T(2,128)S(1)}) custom-call(f32[1]{0:T(128)S(6)} %copy.11.sharp_ref, f32[1]{0:T(128)S(6)} %copy.12.bias_ref, f32[8,128]{1,0:T(8,128)} %bitcast.3, bf16[256,1152]{1,0:T(8,128)(2,1)} %images_hbm.1, bf16[256,1152]{1,0:T(8,128)(2,1)} %texts_hbm.1), custom_call_target="tpu_custom_call" | custom-call | tf_op jit(solution)/shard_map/pairs/pallas_call | solution.py:437
  71.8 1.0 %copy.13 = f32[256,1152]{1,0:T(8,128)} copy(f32[256,1152]{1,0:T(8,128)S(1)} %get-tuple-element.12) | data formatting | bytes 2359296
  72.8 0.8 %copy.14 = bf16[256,1152]{1,0:T(8,128)(2,1)} copy(bf16[256,1152]{1,0:T(8,128)(2,1)S(1)} %get-tuple-element.13) | data formatting | bytes 1179648
  73.6 0.6 copy.15
